TPU v7x, 512 devices: a whole 4x4x16 slice. The times are simulated.
512 devices in a mesh: rep: 16 (over z), ep: 32 (over y, x, core).
Axes of the slice: x: 4, y: 4, z: 16, core: 2. Of those that a mesh axis runs over, the one named last changes fastest.
Arguments:
- tokens: bfloat16 [2048, 4096], P('rep'), may hold values from -6 to 6
- routes: int32 [2048, 2], P('rep'), may hold values from 0 to 7, all different within a row; in each aligned block of 128 rows (0 to 127, 128 to 255, ...) at most 64 rows name the same one
- gates: bfloat16 [2048, 2], P('rep'), may hold values from 0.19921875 to 1
- w_gate: bfloat16 [32, 1792, 4096], P('ep', 'rep'), may hold values from -0.09375 to 0.09375
- w_up: bfloat16 [32, 1792, 4096], P('ep', 'rep'), may hold values from -0.09375 to 0.09375
- direction: bfloat16 [32, 1792, 4096], P('ep', None, 'rep'), may hold values from -32 to 32
Outputs:
- next_direction: bfloat16 [32, 1792, 4096], P('ep', None, 'rep')
- rayleigh: float32 [1], replicated
Inputs may be any that keep to these rules, and one draw needn't show every extreme that they name: `routes`: each row names two different experts. In each aligned block of 128 rows (the tokens of one replica) no expert is named by more than 64 rows, and in some block some expert is named by exactly 64 rows.
All inputs are finite; a program needn't handle non-finite values.
Results may differ from a plain program's by a relative error of at most 0.007.
Values may be sent and summed in bfloat16 or wider, within the bound.
A program may use at most 64 MiB of HBM per device.

v0:
```python
import jax
import jax.numpy as jnp
from jax import lax
from jax.sharding import PartitionSpec as P

D = 4096
FF = 7168
EXPERTS = 8
ITERS = 2
CAP = 64


def own_slots(route_rows, expert, depth):
    pairs = route_rows.reshape(-1)
    hits = (pairs == expert).astype(jnp.int32)
    rank = jnp.cumsum(hits) - hits
    slots = jnp.arange(depth, dtype=jnp.int32)[:, None]
    return ((slots == rank[None, :]) & (hits[None, :] > 0)).astype(jnp.float32)


def on_device(tokens, routes, gates, w_gate, w_up, direction):
    n_rep = lax.axis_size("rep")
    n_ep = lax.axis_size("ep")
    slices = n_ep // EXPERTS
    local = tokens.shape[0]
    depth = CAP
    expert = lax.axis_index("ep") // slices
    route_all = lax.all_gather(routes, "rep", axis=0, tiled=True).reshape(n_rep, local, 2)
    tables = jax.vmap(lambda chosen: own_slots(chosen, expert, depth))(route_all)
    token_map = tables.reshape(n_rep, depth, local, 2).sum(axis=3)
    own_table = lax.dynamic_index_in_dim(tables, lax.axis_index("rep"), 0, keepdims=False)
    own_tokens = own_table.reshape(depth, local, 2).sum(axis=2)
    picked = jnp.dot(
        own_tokens.astype(jnp.bfloat16), tokens, preferred_element_type=jnp.float32
    ).astype(jnp.bfloat16)
    picked_gate = jnp.dot(
        own_table, gates.reshape(-1).astype(jnp.float32), precision=lax.Precision.HIGHEST
    ).astype(jnp.bfloat16)
    rows, rates = (
        lax.all_gather(picked, "rep", axis=0, tiled=True),
        lax.all_gather(picked_gate, "rep", axis=0, tiled=True),
    )
    contract = (((1,), (1,)), ((), ()))
    pre_gate = lax.dot_general(w_gate[0], rows, contract, preferred_element_type=jnp.float32)
    pre_up = lax.dot_general(w_up[0], rows, contract, preferred_element_type=jnp.float32)
    gated = (jax.nn.silu(pre_gate) * pre_up * rates.astype(jnp.float32)[None, :]).astype(
        jnp.bfloat16
    )
    hidden_t = lax.all_gather(gated, "rep", axis=0, tiled=True)
    current = direction[0]
    columns = current.shape[1]
    count = float(EXPERTS * FF * D)
    rayleigh = jnp.zeros((), jnp.float32)
    first_dims = (((0,), (0,)), ((), ()))
    for step in range(ITERS):
        partial_value = lax.dot_general(
            hidden_t, current, first_dims, preferred_element_type=jnp.float32
        ).reshape(n_rep, depth, columns)
        spread = jnp.einsum(
            "rst,rsd->rtd", token_map, partial_value, precision=lax.Precision.HIGHEST
        ).reshape(n_rep * local, columns)
        tangent = lax.psum_scatter(spread, "ep", scatter_dimension=0, tiled=True)
        piece = tangent.astype(jnp.bfloat16)
        sent = lax.all_gather(piece, "ep", axis=0, tiled=True)
        current_f = current.astype(jnp.float32)
        arrived = jnp.einsum(
            "rst,rtd->rsd",
            token_map.astype(jnp.bfloat16),
            sent.reshape(n_rep, local, columns),
            preferred_element_type=jnp.float32,
        ).astype(jnp.bfloat16)
        product = (
            jnp.dot(
                hidden_t,
                arrived.reshape(n_rep * depth, columns),
                preferred_element_type=jnp.float32,
            )
            / n_rep
        )
        energy, cross, square = lax.psum(
            (
                jnp.sum(product * product),
                jnp.sum(current_f * product),
                jnp.sum(current_f * current_f),
            ),
            ("rep", "ep"),
        )
        rayleigh = cross / count / (square / count + 1e-06)
        current = (product * lax.rsqrt(energy / count + 1e-06)).astype(jnp.bfloat16)
    return (current[None], rayleigh.reshape(1))


def solution(mesh):
    return jax.shard_map(
        on_device,
        mesh=mesh,
        in_specs=(
            P("rep", None),
            P("rep", None),
            P("rep", None),
            P("ep", "rep", None),
            P("ep", "rep", None),
            P("ep", None, "rep"),
        ),
        out_specs=(P("ep", None, "rep"), P()),
        check_vma=False,
    )
```

profile of v0, /device:TPU:1, one launch (start us, length us, event | category | flops | bytes accessed | tf_op | source)
XLA Modules:
  0.0 805.5 jit_solution(234640360543273105)
XLA Ops:
  7.2 29.7 %all_gather.18 = s32[2048,2]{0,1:T(2,128)S(1)} all-gather(s32[128,2]{0,1:T(2,128)} %param.7), channel_id=1, replica_groups=mesh['rep'=16,'ep'=32] {'rep'}, dimensions={0}, use_global_device_ids=true | all-gather | bytes 17408 | tf_op jit(solution)/shard_map/all_gather | solution.py:28
  37.0 0.4 copy.50
  37.3 0.6 reshape.108
  38.0 0.5 reshape.109
  38.4 0.6 reduce-window.6
  39.0 0.2 slice_reduce_fusion
  39.3 0.1 bitcast_subtract_fusion.1
  39.3 1.4 fusion
  40.8 0.2 reduce_sum.54
  41.0 1.1 convolution_convert_fusion
  42.1 0.0 all-gather.7.cloned.1.call-start
  42.2 0.1 copy.54
  42.3 0.1 reshape.116
  42.5 1.3 dynamic-slice
  44.4 0.1 fusion.6
  44.5 0.2 dynamic-update-slice
  44.7 20.1 %all-reduce = bf16[1024]{0:T(1024)(128)(2,1)S(1)} all-reduce(bf16[1024]{0:T(1024)(128)(2,1)S(1)} %dynamic-update-slice), channel_id=1, replica_groups=mesh['rep'=16,'ep'=32] {'rep'}, use_global_device_ids=true, to_apply=%add | all-reduce | flops 1024 | bytes 4096
  64.8 86.5 %all-gather.5.cloned.1.call-done = bf16[1024,4096]{1,0:T(8,128)(2,1)} async-done(((bf16[64,4096]{1,0:T(8,128)(2,1)}), bf16[1024,4096]{1,0:T(8,128)(2,1)}) %all-gather.5.cloned.1.call-update) | async-done | bytes 8388624 | tf_op jit(solution)/shard_map/all_gather | solution.py:40
  151.3 6.4 convolution_bitcast_fusion.1
  157.7 3.5 fusion.5
  161.3 0.0 reduce-scatter.3.cloned.1.call-start
  161.3 0.1 copy.56
  161.4 0.1 copy.55
  161.5 0.1 broadcast.47
  161.6 0.1 reshape.99
  161.7 0.1 copy.57
  161.8 0.2 convert_reduce_fusion
  162.1 66.3 %all-gather.7.cloned.1.call-done = bf16[1792,1024]{1,0:T(8,128)(2,1)} async-done(((bf16[112,1024]{1,0:T(8,128)(2,1)}), bf16[1792,1024]{1,0:T(8,128)(2,1)}) %all-gather.7.cloned.1.call-update) | async-done | bytes 3670032 | tf_op jit(solution)/shard_map/all_gather | solution.py:49
  228.3 6.0 copy.60
  234.4 3.2 fusion.9
  237.5 3.2 fusion.20
  240.8 0.0 all-gather.9.cloned.1.call-start
  240.8 105.8 %reduce-scatter.3.cloned.1.call-done = f32[64,256]{1,0:T(8,128)} async-done(((f32[2048,256]{1,0:T(8,128)}), f32[64,256]{1,0:T(8,128)}) %reduce-scatter.3.cloned.1.call-update) | async-done | bytes 65552 | tf_op jit(solution)/shard_map/reduce_scatter | solution.py:62
  346.6 1.5 convert_element_type.87
  348.1 0.2 reduce-scatter.5.cloned.1.call-start
  348.3 61.5 %all-gather.9.cloned.1.call-done = bf16[2048,256]{1,0:T(8,128)(2,1)} async-done(((bf16[64,256]{1,0:T(8,128)(2,1)}), bf16[2048,256]{1,0:T(8,128)(2,1)}) %all-gather.9.cloned.1.call-update) | async-done | bytes 1048592 | tf_op jit(solution)/shard_map/all_gather | solution.py:64
  409.8 1.5 convolution_convert_fusion.2
  411.3 3.8 multiply_reduce_fusion.1
  415.1 103.6 %psum.28 = f32[]{:T(128)} all-reduce(f32[]{:T(128)} %get-tuple-element.8), channel_id=1, replica_groups=mesh['rep'=16,'ep'=32] {'rep','ep'}, use_global_device_ids=true, to_apply=%region_6.7 | all-reduce | flops 1 | bytes 8 | tf_op jit(solution)/shard_map/psum | solution.py:80
  519.4 3.2 fusion.19
  522.6 3.2 fusion.21
  526.0 95.4 %reduce-scatter.5.cloned.1.call-done = f32[64,256]{1,0:T(8,128)} async-done(((f32[2048,256]{1,0:T(8,128)}), f32[64,256]{1,0:T(8,128)}) %reduce-scatter.5.cloned.1.call-update) | async-done | bytes 65552 | tf_op jit(solution)/shard_map/reduce_scatter | solution.py:62
  621.3 1.5 convert_element_type.90
  622.8 61.7 %all-gather.11.cloned.1.call-done = bf16[2048,256]{1,0:T(8,128)(2,1)} async-done(((bf16[64,256]{1,0:T(8,128)(2,1)}), bf16[2048,256]{1,0:T(8,128)(2,1)}) %all-gather.11.cloned.1.call-update) | async-done | bytes 1048592 | tf_op jit(solution)/shard_map/all_gather | solution.py:64
  684.5 1.5 convolution_convert_fusion.1
  686.1 4.6 fusion.1
  690.6 103.8 %all-reduce.1 = (f32[]{:T(128)}, f32[]{:T(128)}, f32[]{:T(128)}) all-reduce(f32[]{:T(128)} %get-tuple-element.3, f32[]{:T(128)} %get-tuple-element.2, f32[]{:T(128)} %get-tuple-element.4), channel_id=1, replica_groups=mesh['rep'=16,'ep'=32] {'rep','ep'}, use_global_device_ids=true, to_apply=%region_9.10 | all-reduce | flops 3 | bytes 24 | tf_op jit(solution)/shard_map/psum | solution.py:80
  796.5 1.1 fusion.8
  (35 shorter events, 0.4 us)
Async XLA Ops:
  7.2 33.8 %copy-start = (bf16[128,4096]{1,0:T(8,128)(2,1)S(1)}, bf16[128,4096]{1,0:T(8,128)(2,1)}, u32[]{:S(2)}) copy-start(bf16[128,4096]{1,0:T(8,128)(2,1)} %param.6) | copy-start | bytes 3145732
  7.2 144.1 %all-gather.5.cloned.1.call-start = ((), (), s32[]{:S(2)}) async-start(), calls=%async_computation.2 | async-start | bytes 8912896 | tf_op jit(solution)/shard_map/all_gather | solution.py:40
  37.9 4.2 copy-start.1
  38.0 113.3 %copy-start.3 = (bf16[1,112,4096]{2,1,0:T(8,128)(2,1)S(1)}, bf16[1,112,4096]{2,1,0:T(8,128)(2,1)}, u32[]{:S(2)}) copy-start(bf16[1,112,4096]{2,1,0:T(8,128)(2,1)} %param.9) | copy-start | bytes 2752516
  42.1 186.2 %all-gather.7.cloned.1.call-start = ((), (), s32[]{:S(2)}) async-start(), calls=%async_computation.3 | async-start | bytes 3899392 | tf_op jit(solution)/shard_map/all_gather | solution.py:49
  151.3 6.4 copy-start.2
  151.3 6.4 copy-start.4
  161.3 185.3 %reduce-scatter.3.cloned.1.call-start = ((), (), s32[]{:S(2)}) async-start(), calls=%async_computation.4 | async-start | bytes 2162688 | tf_op jit(solution)/shard_map/reduce_scatter | solution.py:62
  228.3 6.0 copy-start.5
  240.8 169.0 %all-gather.9.cloned.1.call-start = ((), (), s32[]{:S(2)}) async-start(), calls=%async_computation.5 | async-start | bytes 1081344 | tf_op jit(solution)/shard_map/all_gather | solution.py:64
  348.1 273.2 %reduce-scatter.5.cloned.1.call-start = ((), (), s32[]{:S(2)}) async-start(), calls=%async_computation.6 | async-start | bytes 2162688 | tf_op jit(solution)/shard_map/reduce_scatter | solution.py:62
  415.1 107.5 %copy-start.6 = (f32[1792,256]{1,0:T(8,128)}, f32[1792,256]{1,0:T(8,128)S(1)}, u32[]{:S(2)}) copy-start(f32[1792,256]{1,0:T(8,128)S(1)} %get-tuple-element.9) | copy-start | bytes 5505028
  525.9 158.6 %all-gather.11.cloned.1.call-start = ((), (), s32[]{:S(2)}) async-start(), calls=%async_computation.7 | async-start | bytes 1081344 | tf_op jit(solution)/shard_map/all_gather | solution.py:64
Sparse Core Ops, SparseCore 0:
  42.2 109.0 all-gather.4
  161.4 66.8 all-gather.6
  240.9 105.6 reduce-scatter.2
  350.2 59.5 all-gather.8
  526.0 95.2 reduce-scatter.4
  624.9 59.5 all-gather.10
where the time goes:
time: 806 us
  waiting for transfers between devices  477 us (59%)
  blocking collectives  257 us (32%)
  matrix products  35.4 us (4%)
  between operations  18.9 us (2%)
  local copies, waits for them, and re-layouts  9.84 us (1%)
    psum x2, blocking collectives, on_device(): lax.psum((jnp.sum(product * product), jnp.sum(current_f * product), jnp.s...  207 us
    reduce_scatter x2, waiting for transfers between devices, on_device(): tangent = lax.psum_scatter(spread, 'ep', scatter_dimension=0, tiled=True)  201 us
    all_gather x2, waiting for transfers between devices, on_device(): sent = lax.all_gather(piece, 'ep', axis=0, tiled=True)  123 us
    all_gather x1, waiting for transfers between devices, on_device(): lax.all_gather(picked, 'rep', axis=0, tiled=True)  86.5 us
    all_gather x1, waiting for transfers between devices, on_device(): hidden_t = lax.all_gather(gated, 'rep', axis=0, tiled=True)  66.3 us
    all_gather x1, blocking collectives, on_device(): lax.all_gather(routes, 'rep', axis=0, tiled=True).reshape(n_rep, local, 2)  29.7 us
    unnamed x1, blocking collectives  20.1 us
  transfers between devices with their start and end apart: 6, of which 6 were waited for; matrix products, arithmetic and copies ran while one was open for 0% of the time, Pallas kernels for 0%

commit v1 on v0

v1 whole, which is shorter than its diff:
```python
import functools

import jax
import jax.numpy as jnp
from jax import lax
from jax.experimental import pallas as pl
from jax.experimental.pallas import tpu as pltpu
from jax.sharding import PartitionSpec as P

EXPERTS = 8
CAP = 64
ITERS = 2
LANES = 128
PARTS = 2
F32, BF16 = jnp.float32, jnp.bfloat16


def dot(a, b):
    return jnp.dot(a, b, preferred_element_type=F32)


def dot_nt(a, b):
    return lax.dot_general(a, b, (((1,), (1,)), ((), ())), preferred_element_type=F32)


def active(way, step, part, half):
    if step < half:
        return True
    return (part < PARTS // 2) == (way == 0)


def kernel(
    n_rep, n_ep, units, count,
    rg_ref, tok_ref, wg_ref, wu_ref, dir_ref,
    out_ref, ray_ref,
    wcat, cur0, cur1, rows, rgbuf, hid, hid_t, table, table_t,
    part, swap, snd, rcv, picks, arr, prod,
    red_own, red_sib, red_zsrc, red_z, red_psrc, red_p,
    load_sem, rg_sem, row_sem, sib_sem, hid_sem, swap_sem, a2a_sem, back_sem, fwd_sem,
    rsib_sem, rz_sem, rp_sem,
):
    z = lax.axis_index("rep")
    ep = lax.axis_index("ep")
    chips = n_ep // 2
    per_expert = chips // EXPERTS
    chip, core = ep // 2, lax.rem(ep, 2)
    expert = chip // per_expert
    half = n_rep // 2
    slots = n_rep * CAP
    tok = tok_ref.shape[0]
    width = tok_ref.shape[1] // 2
    piece = width // PARTS
    hpiece = slots // PARTS
    tile = min(256, slots)
    tiles = slots // tile
    sib = {"ep": chip * 2 + 1 - core}
    own_lanes = pl.ds(pl.multiple_of(core * LANES, LANES), LANES)
    other_lanes = pl.ds(pl.multiple_of((1 - core) * LANES, LANES), LANES)

    def remote(src, dst, sems, index, arrive, device):
        return pltpu.make_async_remote_copy(
            src_ref=src, dst_ref=dst,
            send_sem=sems.at[(0, *index)], recv_sem=sems.at[(1, *arrive)],
            device_id=device, device_id_type=pl.DeviceIdType.MESH,
        )

    barrier = pltpu.get_barrier_semaphore()

    @pl.loop(1, n_rep)
    def _(k):
        pl.semaphore_signal(
            barrier, inc=1, device_id={"rep": lax.rem(z + k, n_rep)},
            device_id_type=pl.DeviceIdType.MESH,
        )

    @pl.loop(1, chips)
    def _(k):
        pl.semaphore_signal(
            barrier, inc=1, device_id={"ep": lax.rem(chip + k, chips) * 2 + core},
            device_id_type=pl.DeviceIdType.MESH,
        )

    pl.semaphore_signal(barrier, inc=1, device_id=sib, device_id_type=pl.DeviceIdType.MESH)

    loads = [
        pltpu.make_async_copy(wg_ref, wcat.at[pl.ds(0, units)], load_sem.at[0]),
        pltpu.make_async_copy(wu_ref, wcat.at[pl.ds(LANES, units)], load_sem.at[1]),
        pltpu.make_async_copy(dir_ref, cur0.at[:, pl.ds(0, units)], load_sem.at[2]),
    ]
    for load in loads:
        load.start()
    pad = LANES - units
    wcat[units:LANES, :] = jnp.zeros((pad, wcat.shape[1]), BF16)
    wcat[LANES + units : 2 * LANES, :] = jnp.zeros((pad, wcat.shape[1]), BF16)
    cur0[:, units:LANES, :] = jnp.zeros((n_rep, pad, cur0.shape[2]), BF16)
    hid[:, units:LANES, :] = jnp.zeros((n_rep, pad, slots), BF16)

    before = (
        lax.broadcasted_iota(jnp.int32, (tok, tok), 0)
        < lax.broadcasted_iota(jnp.int32, (tok, tok), 1)
    ).astype(BF16)
    slot_of = lax.broadcasted_iota(jnp.int32, (CAP, tok), 0).astype(F32)

    def slot_table(rg, which):
        hit = jnp.where((rg[0:1] == which) | (rg[1:2] == which), 1.0, 0.0)
        rank = dot(jnp.broadcast_to(hit, (16, tok)).astype(BF16), before)[0:1]
        return jnp.where(slot_of == rank, 1.0, 0.0) * hit

    expert_f = expert.astype(F32)
    own_rg = rg_ref[...]
    own_table = slot_table(own_rg, expert_f).astype(BF16)
    rgbuf[z] = own_rg
    step_w = min(512, width)
    for h in range(2):
        for k in range(width // step_w):
            at = h * width + k * step_w
            rows[h, z, :, k * step_w : (k + 1) * step_w] = dot(
                own_table, tok_ref[:, at : at + step_w]
            ).astype(BF16)

    pl.semaphore_wait(barrier, n_rep - 1 + chips - 1 + 1)

    def block_at(way, step):
        return lax.rem(z + (n_rep - step if way == 0 else step), n_rep)

    def toward(way):
        return {"rep": lax.rem(z + (1 if way == 0 else n_rep - 1), n_rep)}

    def row_copy(way, step, q):
        ref = rows.at[core, block_at(way, step - 1), :, pl.ds(q * piece, piece)]
        i = (way, step - 1, q)
        return remote(ref, ref, row_sem, i, i, toward(way))

    def row_arrival(way, step, q):
        ref = rows.at[core, block_at(way, step), :, pl.ds(q * piece, piece)]
        i = (way, step - 1, q)
        return remote(ref, ref, row_sem, i, i, toward(way))

    def sib_copy(way, step, q):
        ref = rows.at[core, block_at(way, step), :, pl.ds(q * piece, piece)]
        i = (way, step - 1, q)
        return remote(ref, ref, sib_sem, i, i, sib)

    def sib_arrival(way, step, q):
        ref = rows.at[1 - core, block_at(way, step), :, pl.ds(q * piece, piece)]
        i = (way, step - 1, q)
        return remote(ref, ref, sib_sem, i, i, sib)

    order = [
        (step, q, way)
        for step in range(1, half + 1)
        for q in range(PARTS)
        for way in range(2)
        if active(way, step, q, half)
    ]
    for step, q, way in order:
        if step == 1:
            row_copy(way, 1, q).start()

    def rg_copy(k):
        return remote(
            rg_ref, rgbuf.at[z], rg_sem, (lax.rem(z + k, n_rep),), (z,),
            {"rep": lax.rem(z + k, n_rep)},
        )

    def rg_arrival(k):
        b = lax.rem(z + k, n_rep)
        return remote(rg_ref, rgbuf.at[b], rg_sem, (b,), (b,), {"rep": b})

    @pl.loop(1, n_rep)
    def _(k):
        rg_copy(k).start()

    for step, q, way in order:
        row_arrival(way, step, q).wait_recv()
        if step < half and active(way, step + 1, q, half):
            row_copy(way, step + 1, q).start()
        sib_copy(way, step, q).start()
        if (step, q, way) == (1, 0, 0):

            @pl.loop(1, n_rep)
            def _(k):
                rg_arrival(k).wait_recv()

            owned = rgbuf[chip]
            for e in range(EXPERTS):
                t = slot_table(owned, jnp.float32(e))
                table_t[e * CAP : (e + 1) * CAP, :] = t.astype(BF16)
                tt = jnp.transpose(t, (1, 0))
                table[e] = jnp.concatenate([tt] * per_expert, axis=1).astype(BF16)
            for load in loads:
                load.wait()

    for step, q, way in order:
        sib_arrival(way, step, q).wait_recv()

    def hid_copy(way, step, q):
        ref = hid.at[block_at(way, step - 1), pl.ds(0, units), pl.ds(q * hpiece, hpiece)]
        i = (way, step - 1, q)
        return remote(ref, ref, hid_sem, i, i, toward(way))

    def hid_arrival(way, step, q):
        ref = hid.at[block_at(way, step), pl.ds(0, units), pl.ds(q * hpiece, hpiece)]
        i = (way, step - 1, q)
        return remote(ref, ref, hid_sem, i, i, toward(way))

    unit_lanes = pl.ds(pl.multiple_of(z * LANES, LANES), LANES)
    per_tile = tile // CAP
    for m in range(tiles):
        pre = jnp.zeros((tile, 2 * LANES), F32)
        for h in range(2):
            x = rows[h, m * per_tile : (m + 1) * per_tile].reshape(tile, width)
            pre = pre + dot_nt(x, wcat[:, h * width : (h + 1) * width])
        rates = []
        for b in range(m * per_tile, (m + 1) * per_tile):
            rg = rgbuf[b]
            g = jnp.where(rg[0:1] == expert_f, rg[2:3], 0.0) + jnp.where(
                rg[1:2] == expert_f, rg[3:4], 0.0
            )
            rates.append(jnp.sum(slot_table(rg, expert_f) * g, axis=1, keepdims=True))
        rate = jnp.concatenate(rates, axis=0)
        pg, pu = pre[:, :LANES], pre[:, LANES:]
        gated = pg * (1.0 / (1.0 + jnp.exp(-pg))) * pu * rate
        hid_t[m * tile : (m + 1) * tile, unit_lanes] = gated.astype(BF16)
        hid[z, 0:units, m * tile : (m + 1) * tile] = jnp.transpose(gated, (1, 0))[
            :units
        ].astype(BF16)
        if (m + 1) * tile % hpiece == 0:
            q = (m + 1) * tile // hpiece - 1
            for way in range(2):
                if active(way, 1, q, half):
                    hid_copy(way, 1, q).start()
        elif tiles == 1:
            for q in range(PARTS):
                for way in range(2):
                    if active(way, 1, q, half):
                        hid_copy(way, 1, q).start()

    for step, q, way in order:
        hid_arrival(way, step, q).wait_recv()
        if step < half and active(way, step + 1, q, half):
            hid_copy(way, step + 1, q).start()
        b = block_at(way, step)
        lanes = pl.ds(pl.multiple_of(b * LANES, LANES), LANES)
        hid_t[q * hpiece : (q + 1) * hpiece, lanes] = jnp.transpose(
            hid[b, :, q * hpiece : (q + 1) * hpiece], (1, 0)
        )

    def red_sib_copy(it):
        return remote(red_own.at[it], red_sib.at[it], rsib_sem, (it,), (it,), sib)

    def red_z_copy(it, k):
        b = lax.rem(z + k, n_rep)
        return remote(red_zsrc.at[it], red_z.at[it, z], rz_sem, (it, b), (it, z), {"rep": b})

    def red_z_arrival(it, k):
        b = lax.rem(z + k, n_rep)
        return remote(red_zsrc.at[it], red_z.at[it, b], rz_sem, (it, b), (it, b), {"rep": b})

    def red_p_copy(it, k):
        j = lax.rem(chip + k, chips)
        return remote(
            red_psrc.at[it], red_p.at[it, chip], rp_sem, (it, j), (it, chip),
            {"ep": j * 2 + core},
        )

    def red_p_arrival(it, k):
        j = lax.rem(chip + k, chips)
        return remote(
            red_psrc.at[it], red_p.at[it, j], rp_sem, (it, j), (it, j), {"ep": j * 2 + core}
        )

    def reduce_z(it):
        red_sib_copy(it).wait_recv()
        both = red_own[it] + red_sib[it]
        red_zsrc[it] = both
        red_z[it, z] = both

        @pl.loop(1, n_rep)
        def _(k):
            red_z_copy(it, k).start()

    def reduce_plane(it):
        @pl.loop(1, n_rep)
        def _(k):
            red_z_arrival(it, k).wait_recv()

        column = jnp.sum(red_z[it], axis=0)
        red_psrc[it] = column
        red_p[it, chip] = column

        @pl.loop(1, chips)
        def _(k):
            red_p_copy(it, k).start()

    def reduce_end(it):
        @pl.loop(1, chips)
        def _(k):
            red_p_arrival(it, k).wait_recv()

        return jnp.sum(jnp.sum(red_p[it], axis=0), axis=1, keepdims=True)

    row_y, row_x = chip // per_tile, lax.rem(chip, per_tile)

    def tile_at(i):
        return lax.rem(row_y + i, tiles)

    def swap_copy(it, i):
        at = pl.ds(pl.multiple_of(tile_at(i) * tile, tile), tile)
        return remote(
            part.at[it, at, other_lanes], swap.at[it, at], swap_sem, (it, i), (it, i), sib
        )

    def a2a_copy(it, j):
        return remote(
            snd.at[it, j], rcv.at[it, chip], a2a_sem, (it, j), (it, chip),
            {"ep": j * 2 + core},
        )

    def a2a_arrival(it, k):
        j = lax.rem(chip + k, chips)
        return remote(
            snd.at[it, j], rcv.at[it, j], a2a_sem, (it, j), (it, j), {"ep": j * 2 + core}
        )

    def slot_rows(j):
        return pl.ds(pl.multiple_of(j * CAP, CAP), CAP)

    def back_copy(it, k):
        j = lax.rem(chip + k, chips)
        return remote(
            picks.at[it, j // per_expert], arr.at[it, slot_rows(chip), own_lanes],
            back_sem, (it, j), (it, chip), {"ep": j * 2 + core},
        )

    def back_arrival(it, k):
        j = lax.rem(chip + k, chips)
        return remote(
            picks.at[it, j // per_expert], arr.at[it, slot_rows(j), own_lanes],
            back_sem, (it, j), (it, j), {"ep": j * 2 + core},
        )

    def fwd_copy(it, k):
        j = lax.rem(chip + k, chips)
        ref = arr.at[it, slot_rows(j), own_lanes]
        return remote(ref, ref, fwd_sem, (it, j), (it, j), sib)

    def fwd_arrival(it, k):
        j = lax.rem(chip + k, chips)
        ref = arr.at[it, slot_rows(j), other_lanes]
        return remote(ref, ref, fwd_sem, (it, j), (it, j), sib)

    groups = n_rep * LANES // 256
    columns = cur0.shape[2]

    def fold(v):
        s = jnp.sum(v.reshape(v.shape[0] // 8, 8, columns), axis=0)
        return s[:, :LANES] + s[:, LANES:]

    scale = None
    for it in range(ITERS):
        source = cur0 if it == 0 else cur1
        for i in range(tiles):
            at = pl.ds(pl.multiple_of(tile_at(i) * tile, tile), tile)
            part[it, at, :] = dot(
                hid_t[at, :], source[...].reshape(n_rep * LANES, columns)
            )
            swap_copy(it, i).start()
            if it == 1 and i == 0:
                reduce_z(0)
        if it == 1:
            reduce_plane(0)
        for i in range(tiles):
            swap_copy(it, i).wait_recv()
            m = tile_at(i)
            at = pl.ds(pl.multiple_of(m * tile, tile), tile)
            own = (part[it, at, own_lanes] + swap[it, at]).astype(BF16)
            snd[it, pl.ds(m * per_tile, per_tile)] = own.reshape(per_tile, CAP, LANES)
            if i == 0:
                rcv[it, chip] = snd[it, chip]
            for k in range(1 if i == 0 else 0, per_tile):
                a2a_copy(it, m * per_tile + lax.rem(row_x + k, per_tile)).start()

        @pl.loop(1, chips)
        def _(k):
            a2a_arrival(it, k).wait_recv()

        tangent = jnp.zeros((tok, LANES), F32)
        for e in range(EXPERTS):
            got = rcv[it, e * per_expert : (e + 1) * per_expert].reshape(
                per_expert * CAP, LANES
            )
            tangent = tangent + dot(table[e], got)
        if it == 1:
            scale = lax.rsqrt(reduce_end(0)[0:1] / count + 1e-06)
            tangent = tangent * scale
        sent = tangent.astype(BF16)
        picks[it] = dot(table_t[...], sent).astype(BF16).reshape(EXPERTS, CAP, LANES)
        arr[it, slot_rows(chip), own_lanes] = picks[it, expert]
        fwd_copy(it, 0).start()

        @pl.loop(1, chips)
        def _(k):
            back_copy(it, k).start()

        @pl.loop(1, chips)
        def _(k):
            back_arrival(it, k).wait_recv()
            fwd_copy(it, k).start()

        @pl.loop(0, chips)
        def _(k):
            fwd_arrival(it, k).wait_recv()

        energy = jnp.zeros((8, LANES), F32)
        cross, square = energy, energy
        for g in range(groups):
            x = hid[2 * g : 2 * g + 2].reshape(256, slots)
            p = dot(x, arr[it]) / n_rep
            energy = energy + fold(p * p)
            if it == 0:
                cur1[2 * g : 2 * g + 2] = p.astype(BF16).reshape(2, LANES, columns)
            else:
                prod[2 * g : 2 * g + 2] = p.reshape(2, LANES, columns)
                c = cur1[2 * g : 2 * g + 2].reshape(256, columns).astype(F32) * scale
                cross = cross + fold(c * p)
                square = square + fold(c * c)
        red_own[it] = jnp.concatenate(
            [jnp.sum(v, axis=0, keepdims=True) for v in (energy, cross, square)]
            + [jnp.zeros((5, LANES), F32)],
            axis=0,
        )
        red_sib_copy(it).start()

    reduce_z(1)
    reduce_plane(1)
    total = reduce_end(1)
    ray_ref[...] = jnp.broadcast_to(
        total[1:2] / count / (total[2:3] / count + 1e-06), (8, LANES)
    )
    last = lax.rsqrt(total[0:1] / count + 1e-06)
    for g in range(n_rep):
        out_ref[g] = (prod[g, :units, :] * last).astype(BF16)

    @pl.loop(1, n_rep)
    def _(k):
        rg_copy(k).wait_send()
        for it in range(ITERS):
            red_z_copy(it, k).wait_send()

    for step, q, way in order:
        row_copy(way, step, q).wait_send()
        sib_copy(way, step, q).wait_send()
        hid_copy(way, step, q).wait_send()
    for it in range(ITERS):
        red_sib_copy(it).wait_send()
        for i in range(tiles):
            swap_copy(it, i).wait_send()

        @pl.loop(1, chips)
        def _(k):
            a2a_copy(it, lax.rem(chip + k, chips)).wait_send()
            back_copy(it, k).wait_send()
            red_p_copy(it, k).wait_send()

        @pl.loop(0, chips)
        def _(k):
            fwd_copy(it, k).wait_send()


def on_device(tokens, routes, gates, w_gate, w_up, direction):
    n_rep = lax.axis_size("rep")
    n_ep = lax.axis_size("ep")
    chips = n_ep // 2
    tok, depth = tokens.shape
    units, inner = w_gate.shape[1], direction.shape[1]
    columns = direction.shape[2]
    slots = n_rep * CAP
    half = n_rep // 2
    width = depth // 2
    count = float(n_rep * n_ep * inner * columns)
    rg = jnp.concatenate(
        [routes.T.astype(F32), gates.T.astype(F32), jnp.zeros((4, tok), F32)], axis=0
    )
    dma = pltpu.SemaphoreType.DMA
    per_expert = chips // EXPERTS
    out, ray = pl.pallas_call(
        functools.partial(kernel, n_rep, n_ep, units, count),
        out_shape=(
            jax.ShapeDtypeStruct((n_rep, units, columns), BF16),
            jax.ShapeDtypeStruct((8, LANES), F32),
        ),
        in_specs=[
            pl.BlockSpec(memory_space=pltpu.VMEM),
            pl.BlockSpec(memory_space=pltpu.VMEM),
            pl.BlockSpec(memory_space=pl.ANY),
            pl.BlockSpec(memory_space=pl.ANY),
            pl.BlockSpec(memory_space=pl.ANY),
        ],
        out_specs=(
            pl.BlockSpec(memory_space=pltpu.VMEM),
            pl.BlockSpec(memory_space=pltpu.VMEM),
        ),
        scratch_shapes=[
            pltpu.VMEM((2 * LANES, depth), BF16),
            pltpu.VMEM((n_rep, LANES, columns), BF16),
            pltpu.VMEM((n_rep, LANES, columns), BF16),
            pltpu.VMEM((2, n_rep, CAP, width), BF16),
            pltpu.VMEM((n_rep, 8, tok), F32),
            pltpu.VMEM((n_rep, LANES, slots), BF16),
            pltpu.VMEM((slots, n_rep * LANES), BF16),
            pltpu.VMEM((EXPERTS, tok, per_expert * CAP), BF16),
            pltpu.VMEM((EXPERTS * CAP, tok), BF16),
            pltpu.VMEM((ITERS, slots, columns), F32),
            pltpu.VMEM((ITERS, slots, LANES), F32),
            pltpu.VMEM((ITERS, chips, CAP, LANES), BF16),
            pltpu.VMEM((ITERS, chips, CAP, LANES), BF16),
            pltpu.VMEM((ITERS, EXPERTS, CAP, LANES), BF16),
            pltpu.VMEM((ITERS, slots, columns), BF16),
            pltpu.VMEM((n_rep, LANES, columns), F32),
            pltpu.VMEM((ITERS, 8, LANES), F32),
            pltpu.VMEM((ITERS, 8, LANES), F32),
            pltpu.VMEM((ITERS, 8, LANES), F32),
            pltpu.VMEM((ITERS, n_rep, 8, LANES), F32),
            pltpu.VMEM((ITERS, 8, LANES), F32),
            pltpu.VMEM((ITERS, chips, 8, LANES), F32),
            dma((3,)),
            dma((2, n_rep)),
            dma((2, 2, half, PARTS)),
            dma((2, 2, half, PARTS)),
            dma((2, 2, half, PARTS)),
            dma((2, ITERS, max(1, slots // 256))),
            dma((2, ITERS, chips)),
            dma((2, ITERS, chips)),
            dma((2, ITERS, chips)),
            dma((2, ITERS)),
            dma((2, ITERS, n_rep)),
            dma((2, ITERS, chips)),
        ],
        compiler_params=pltpu.CompilerParams(
            collective_id=0, has_side_effects=True, vmem_limit_bytes=56 * 2**20
        ),
    )(rg, tokens, w_gate[0], w_up[0], direction[0].reshape(n_rep, units, columns))
    return out.reshape(1, inner, columns), ray[0, :1]


def solution(mesh):
    return jax.shard_map(
        on_device,
        mesh=mesh,
        in_specs=(
            P("rep", None),
            P("rep", None),
            P("rep", None),
            P("ep", "rep", None),
            P("ep", "rep", None),
            P("ep", None, "rep"),
        ),
        out_specs=(P("ep", None, "rep"), P()),
        check_vma=False,
    )
```

time: 806 us -> 185 us (0.23)
  waiting for transfers between devices: 477 us -> 0 us
  blocking collectives: 257 us -> 0 us
  Pallas kernels: 0 us -> 178 us
  matrix products: 35.4 us -> 0 us
  between operations: 18.9 us -> 0.66 us
    all_gather x4 -> x0, waiting for transfers between devices: 276 us -> none  [the longest x2 123 us: on_device(): sent = lax.all_gather(piece, 'ep', axis=0, tiled=True)]
    psum x2 -> x0, blocking collectives: 207 us -> none  [on_device(): lax.psum((jnp.sum(product * product), jnp.sum(current_f * product), jnp.s...]
    reduce_scatter x2 -> x0, waiting for transfers between devices: 201 us -> none  [on_device(): tangent = lax.psum_scatter(spread, 'ep', scatter_dimension=0, tiled=True)]
    pallas_call x0 -> x1, Pallas kernels: none -> 178 us  [on_device(): pl.pallas_call(functools.partial(kernel, n_rep, n_ep, units, count), out_...]
    dot_general x12 -> x0, matrix products: 35.4 us -> none  [the longest x2 8.33 us: on_device(): jnp.dot(hidden_t, arrived.reshape(n_rep * depth, columns), preferred_elem...]
    all_gather x1 -> x0, blocking collectives: 29.7 us -> none  [on_device(): lax.all_gather(routes, 'rep', axis=0, tiled=True).reshape(n_rep, local, 2)]
    unnamed x1 -> x0, blocking collectives: 20.1 us -> none
  transfers between devices with their start and end apart: 6 -> 0, of which waited for: 6 -> 0; matrix products, arithmetic and copies ran while one was open for 0% -> 0% of each run, Pallas kernels for 0% -> 0%
where the time goes in v1:
time: 185 us; the launch traced here: 184 us
  Pallas kernels  178 us (96%)
  local copies, waits for them, and re-layouts  4.67 us (3%)
    pallas_call x1, Pallas kernels, on_device(): pl.pallas_call(functools.partial(kernel, n_rep, n_ep, units, count), out_...  178 us

profile of v1, /device:TPU:1, one launch (start us, length us, event | category | flops | bytes accessed | tf_op | source)
XLA Modules:
  0.0 183.6 jit_solution(6220257950707108967)
XLA Ops:
  0.6 0.0 copy-start
  0.7 0.1 pad.2.clone
  0.7 0.6 copy-done
  1.3 0.0 copy-start.1
  1.3 0.7 copy-done.1
  2.0 0.7 maximum_maximum_fusion.rg_ref
  2.6 177.6 %shard_map.77 = (bf16[16,112,256]{2,1,0:T(8,128)(2,1)}, f32[8,128]{1,0:T(8,128)}) custom-call(f32[8,128]{1,0:T(8,128)} %maximum_maximum_fusion.rg_ref, bf16[128,4096]{1,0:T(8,128)(2,1)} %tok_ref.1, bf16[112,4096]{1,0:T(8,128)(2,1)} %bitcast.10, bf16[112,4096]{1,0:T(8,128)(2,1)} %bitcast.11, bf16[16,112,256]{2,1,0:T(8,128)(2,1)} %bitcast.12), custom_call_target="tpu_custom_call" | custom-call | tf_op jit(solution)/shard_map/pallas_call | solution.py:487
  180.3 1.2 slice.3
  181.4 2.2 %copy.9 = bf16[1,1792,256]{2,1,0:T(8,128)(2,1)} copy(bf16[1,1792,256]{2,1,0:T(8,128)(2,1)} %bitcast.9) | data formatting | bytes 1835008
  (3 shorter events, 0.0 us)
Async XLA Ops:
  0.6 0.7 copy-start
  1.3 0.7 copy-start.1

commit v2 on v1

--- a/solution.py
+++ b/solution.py
@@ -11,7 +11,7 @@
 CAP = 64
 ITERS = 2
 LANES = 128
-PARTS = 2
+PARTS = 4
 F32, BF16 = jnp.float32, jnp.bfloat16
 
 
@@ -31,13 +31,13 @@
 
 def kernel(
     n_rep, n_ep, units, count,
-    rg_ref, tok_ref, wg_ref, wu_ref, dir_ref,
-    out_ref, ray_ref,
+    routes_ref, gates_ref, tok_ref, wg_ref, wu_ref, dir_ref,
+    out_ref, scale_ref, ray_ref,
     wcat, cur0, cur1, rows, rgbuf, hid, hid_t, table, table_t,
-    part, swap, snd, rcv, picks, arr, prod,
-    red_own, red_sib, red_zsrc, red_z, red_psrc, red_p,
-    load_sem, rg_sem, row_sem, sib_sem, hid_sem, swap_sem, a2a_sem, back_sem, fwd_sem,
-    rsib_sem, rz_sem, rp_sem,
+    rates, part, swap, snd, rcv, picks, arr,
+    red_own, red_z, red_psrc, red_p,
+    load_sem, rg_sem, row_sem, pair_sem, sib_sem, hid_sem, swap_sem, a2a_sem, back_sem, fwd_sem,
+    rz_sem, rp_sem,
 ):
     z = lax.axis_index("rep")
     ep = lax.axis_index("ep")
@@ -49,11 +49,13 @@
     slots = n_rep * CAP
     tok = tok_ref.shape[0]
     width = tok_ref.shape[1] // 2
-    piece = width // PARTS
+    third = width // 3 // LANES * LANES
+    parity = lax.rem(chip, 2)
     hpiece = slots // PARTS
     tile = min(256, slots)
     tiles = slots // tile
     sib = {"ep": chip * 2 + 1 - core}
+    pair = {"ep": (chip + 1 - 2 * parity) * 2 + core}
     own_lanes = pl.ds(pl.multiple_of(core * LANES, LANES), LANES)
     other_lanes = pl.ds(pl.multiple_of((1 - core) * LANES, LANES), LANES)
 
@@ -73,14 +75,12 @@
             device_id_type=pl.DeviceIdType.MESH,
         )
 
-    @pl.loop(1, chips)
+    @pl.loop(1, n_ep)
     def _(k):
         pl.semaphore_signal(
-            barrier, inc=1, device_id={"ep": lax.rem(chip + k, chips) * 2 + core},
+            barrier, inc=1, device_id={"ep": lax.rem(ep + k, n_ep)},
             device_id_type=pl.DeviceIdType.MESH,
         )
-
-    pl.semaphore_signal(barrier, inc=1, device_id=sib, device_id_type=pl.DeviceIdType.MESH)
 
     loads = [
         pltpu.make_async_copy(wg_ref, wcat.at[pl.ds(0, units)], load_sem.at[0]),
@@ -107,7 +107,9 @@
         return jnp.where(slot_of == rank, 1.0, 0.0) * hit
 
     expert_f = expert.astype(F32)
-    own_rg = rg_ref[...]
+    own_rg = jnp.concatenate(
+        [routes_ref[...].astype(F32), gates_ref[...].astype(F32), jnp.zeros((4, tok), F32)], axis=0
+    )
     own_table = slot_table(own_rg, expert_f).astype(BF16)
     rgbuf[z] = own_rg
     step_w = min(512, width)
@@ -118,7 +120,7 @@
                 own_table, tok_ref[:, at : at + step_w]
             ).astype(BF16)
 
-    pl.semaphore_wait(barrier, n_rep - 1 + chips - 1 + 1)
+    pl.semaphore_wait(barrier, n_rep - 1 + n_ep - 1)
 
     def block_at(way, step):
         return lax.rem(z + (n_rep - step if way == 0 else step), n_rep)
@@ -126,25 +128,54 @@
     def toward(way):
         return {"rep": lax.rem(z + (1 if way == 0 else n_rep - 1), n_rep)}
 
+    def rows_of(q):
+        return pl.ds(q % 2 * (CAP // 2), CAP // 2)
+
+    def lanes_of(q):
+        if q // 2 == 1:
+            return pl.ds(2 * third, width - 2 * third)
+        first = parity if q // 2 == 0 else 1 - parity
+        return pl.ds(pl.multiple_of(first * third, LANES), third)
+
     def row_copy(way, step, q):
-        ref = rows.at[core, block_at(way, step - 1), :, pl.ds(q * piece, piece)]
+        ref = rows.at[core, block_at(way, step - 1), rows_of(q), lanes_of(q)]
         i = (way, step - 1, q)
         return remote(ref, ref, row_sem, i, i, toward(way))
 
     def row_arrival(way, step, q):
-        ref = rows.at[core, block_at(way, step), :, pl.ds(q * piece, piece)]
+        ref = rows.at[core, block_at(way, step), rows_of(q), lanes_of(q)]
         i = (way, step - 1, q)
         return remote(ref, ref, row_sem, i, i, toward(way))
 
+    def pair_copy(way, step, q):
+        ref = rows.at[core, block_at(way, step), rows_of(q), lanes_of(q)]
+        i = (way, step - 1, q)
+        return remote(ref, ref, pair_sem, i, i, pair)
+
+    def pair_arrival(way, step, q):
+        ref = rows.at[core, block_at(way, step), rows_of(q), lanes_of(q + 4)]
+        i = (way, step - 1, q)
+        return remote(ref, ref, pair_sem, i, i, pair)
+
     def sib_copy(way, step, q):
-        ref = rows.at[core, block_at(way, step), :, pl.ds(q * piece, piece)]
+        ref = rows.at[core, block_at(way, step), rows_of(q), lanes_of(q)]
         i = (way, step - 1, q)
         return remote(ref, ref, sib_sem, i, i, sib)
 
     def sib_arrival(way, step, q):
-        ref = rows.at[1 - core, block_at(way, step), :, pl.ds(q * piece, piece)]
+        ref = rows.at[1 - core, block_at(way, step), rows_of(q), lanes_of(q)]
         i = (way, step - 1, q)
         return remote(ref, ref, sib_sem, i, i, sib)
+
+    def rg_copy(way, step):
+        ref = rgbuf.at[block_at(way, step - 1)]
+        i = (way, step - 1)
+        return remote(ref, ref, rg_sem, i, i, toward(way))
+
+    def rg_arrival(way, step):
+        ref = rgbuf.at[block_at(way, step)]
+        i = (way, step - 1)
+        return remote(ref, ref, rg_sem, i, i, toward(way))
 
     order = [
         (step, q, way)
@@ -153,46 +184,49 @@
         for way in range(2)
         if active(way, step, q, half)
     ]
+    passed = [(step, q, way) for step, q, way in order if q < 2]
+    whole = [(step, way) for step, q, way in passed if q == 0]
+    for way in range(2):
+        if active(way, 1, 0, half):
+            rg_copy(way, 1).start()
     for step, q, way in order:
         if step == 1:
             row_copy(way, 1, q).start()
 
-    def rg_copy(k):
-        return remote(
-            rg_ref, rgbuf.at[z], rg_sem, (lax.rem(z + k, n_rep),), (z,),
-            {"rep": lax.rem(z + k, n_rep)},
-        )
-
-    def rg_arrival(k):
-        b = lax.rem(z + k, n_rep)
-        return remote(rg_ref, rgbuf.at[b], rg_sem, (b,), (b,), {"rep": b})
-
-    @pl.loop(1, n_rep)
-    def _(k):
-        rg_copy(k).start()
-
+    def to_sibling(step, q, way):
+        pair_arrival(way, step, q).wait_recv()
+        sib_copy(way, step, q + 4).start()
+
+    late = list(passed)
     for step, q, way in order:
         row_arrival(way, step, q).wait_recv()
         if step < half and active(way, step + 1, q, half):
             row_copy(way, step + 1, q).start()
+        if q < 2:
+            pair_copy(way, step, q).start()
+        if q == 0:
+            rg_arrival(way, step).wait_recv()
+            if step < half and active(way, step + 1, 0, half):
+                rg_copy(way, step + 1).start()
         sib_copy(way, step, q).start()
-        if (step, q, way) == (1, 0, 0):
-
-            @pl.loop(1, n_rep)
-            def _(k):
-                rg_arrival(k).wait_recv()
-
-            owned = rgbuf[chip]
-            for e in range(EXPERTS):
-                t = slot_table(owned, jnp.float32(e))
-                table_t[e * CAP : (e + 1) * CAP, :] = t.astype(BF16)
-                tt = jnp.transpose(t, (1, 0))
-                table[e] = jnp.concatenate([tt] * per_expert, axis=1).astype(BF16)
-            for load in loads:
-                load.wait()
-
+        if q >= 2 and late and late[0][0] < step:
+            to_sibling(*late.pop(0))
+
+    for b in range(n_rep):
+        rg = rgbuf[b]
+        g = jnp.where(rg[0:1] == expert_f, rg[2:3], 0.0) + jnp.where(
+            rg[1:2] == expert_f, rg[3:4], 0.0
+        )
+        rate = jnp.sum(slot_table(rg, expert_f) * g, axis=1, keepdims=True)
+        rates[b * CAP : (b + 1) * CAP] = jnp.broadcast_to(rate, (CAP, LANES))
+    for load in loads:
+        load.wait()
+    for step, q, way in late:
+        to_sibling(step, q, way)
     for step, q, way in order:
         sib_arrival(way, step, q).wait_recv()
+    for step, q, way in passed:
+        sib_arrival(way, step, q + 4).wait_recv()
 
     def hid_copy(way, step, q):
         ref = hid.at[block_at(way, step - 1), pl.ds(0, units), pl.ds(q * hpiece, hpiece)]
@@ -211,30 +245,16 @@
         for h in range(2):
             x = rows[h, m * per_tile : (m + 1) * per_tile].reshape(tile, width)
             pre = pre + dot_nt(x, wcat[:, h * width : (h + 1) * width])
-        rates = []
-        for b in range(m * per_tile, (m + 1) * per_tile):
-            rg = rgbuf[b]
-            g = jnp.where(rg[0:1] == expert_f, rg[2:3], 0.0) + jnp.where(
-                rg[1:2] == expert_f, rg[3:4], 0.0
-            )
-            rates.append(jnp.sum(slot_table(rg, expert_f) * g, axis=1, keepdims=True))
-        rate = jnp.concatenate(rates, axis=0)
         pg, pu = pre[:, :LANES], pre[:, LANES:]
-        gated = pg * (1.0 / (1.0 + jnp.exp(-pg))) * pu * rate
+        gated = pg * (1.0 / (1.0 + jnp.exp(-pg))) * pu * rates[m * tile : (m + 1) * tile]
         hid_t[m * tile : (m + 1) * tile, unit_lanes] = gated.astype(BF16)
         hid[z, 0:units, m * tile : (m + 1) * tile] = jnp.transpose(gated, (1, 0))[
             :units
         ].astype(BF16)
-        if (m + 1) * tile % hpiece == 0:
-            q = (m + 1) * tile // hpiece - 1
+        for q in range(m * tile // hpiece, (m + 1) * tile // hpiece):
             for way in range(2):
                 if active(way, 1, q, half):
                     hid_copy(way, 1, q).start()
-        elif tiles == 1:
-            for q in range(PARTS):
-                for way in range(2):
-                    if active(way, 1, q, half):
-                        hid_copy(way, 1, q).start()
 
     for step, q, way in order:
         hid_arrival(way, step, q).wait_recv()
@@ -246,35 +266,24 @@
             hid[b, :, q * hpiece : (q + 1) * hpiece], (1, 0)
         )
 
-    def red_sib_copy(it):
-        return remote(red_own.at[it], red_sib.at[it], rsib_sem, (it,), (it,), sib)
-
     def red_z_copy(it, k):
         b = lax.rem(z + k, n_rep)
-        return remote(red_zsrc.at[it], red_z.at[it, z], rz_sem, (it, b), (it, z), {"rep": b})
+        return remote(red_own.at[it], red_z.at[it, z], rz_sem, (it, b), (it, z), {"rep": b})
 
     def red_z_arrival(it, k):
         b = lax.rem(z + k, n_rep)
-        return remote(red_zsrc.at[it], red_z.at[it, b], rz_sem, (it, b), (it, b), {"rep": b})
+        return remote(red_own.at[it], red_z.at[it, b], rz_sem, (it, b), (it, b), {"rep": b})
 
     def red_p_copy(it, k):
-        j = lax.rem(chip + k, chips)
-        return remote(
-            red_psrc.at[it], red_p.at[it, chip], rp_sem, (it, j), (it, chip),
-            {"ep": j * 2 + core},
-        )
+        j = lax.rem(ep + k, n_ep)
+        return remote(red_psrc.at[it], red_p.at[it, ep], rp_sem, (it, j), (it, ep), {"ep": j})
 
     def red_p_arrival(it, k):
-        j = lax.rem(chip + k, chips)
-        return remote(
-            red_psrc.at[it], red_p.at[it, j], rp_sem, (it, j), (it, j), {"ep": j * 2 + core}
-        )
+        j = lax.rem(ep + k, n_ep)
+        return remote(red_psrc.at[it], red_p.at[it, j], rp_sem, (it, j), (it, j), {"ep": j})
 
     def reduce_z(it):
-        red_sib_copy(it).wait_recv()
-        both = red_own[it] + red_sib[it]
-        red_zsrc[it] = both
-        red_z[it, z] = both
+        red_z[it, z] = red_own[it]
 
         @pl.loop(1, n_rep)
         def _(k):
@@ -287,14 +296,14 @@
 
         column = jnp.sum(red_z[it], axis=0)
         red_psrc[it] = column
-        red_p[it, chip] = column
-
-        @pl.loop(1, chips)
+        red_p[it, ep] = column
+
+        @pl.loop(1, n_ep)
         def _(k):
             red_p_copy(it, k).start()
 
     def reduce_end(it):
-        @pl.loop(1, chips)
+        @pl.loop(1, n_ep)
         def _(k):
             red_p_arrival(it, k).wait_recv()
 
@@ -366,10 +375,6 @@
                 hid_t[at, :], source[...].reshape(n_rep * LANES, columns)
             )
             swap_copy(it, i).start()
-            if it == 1 and i == 0:
-                reduce_z(0)
-        if it == 1:
-            reduce_plane(0)
         for i in range(tiles):
             swap_copy(it, i).wait_recv()
             m = tile_at(i)
@@ -381,6 +386,14 @@
             for k in range(1 if i == 0 else 0, per_tile):
                 a2a_copy(it, m * per_tile + lax.rem(row_x + k, per_tile)).start()
 
+        if it == 0:
+            owned = rgbuf[chip]
+            for e in range(EXPERTS):
+                t = slot_table(owned, jnp.float32(e))
+                table_t[e * CAP : (e + 1) * CAP, :] = t.astype(BF16)
+                tt = jnp.transpose(t, (1, 0))
+                table[e] = jnp.concatenate([tt] * per_expert, axis=1).astype(BF16)
+
         @pl.loop(1, chips)
         def _(k):
             a2a_arrival(it, k).wait_recv()
@@ -391,9 +404,6 @@
                 per_expert * CAP, LANES
             )
             tangent = tangent + dot(table[e], got)
-        if it == 1:
-            scale = lax.rsqrt(reduce_end(0)[0:1] / count + 1e-06)
-            tangent = tangent * scale
         sent = tangent.astype(BF16)
         picks[it] = dot(table_t[...], sent).astype(BF16).reshape(EXPERTS, CAP, LANES)
         arr[it, slot_rows(chip), own_lanes] = picks[it, expert]
@@ -403,25 +413,35 @@
         def _(k):
             back_copy(it, k).start()
 
+        if it == 1:
+            reduce_plane(0)
+
         @pl.loop(1, chips)
         def _(k):
             back_arrival(it, k).wait_recv()
             fwd_copy(it, k).start()
 
+        rest = 1.0 / n_rep
+        if it == 1:
+            scale = lax.rsqrt(reduce_end(0)[0:1] / count + 1e-06)
+            power = jnp.exp2(jnp.floor(jnp.log2(scale))).astype(BF16)
+            rest = scale / power.astype(F32) * rest
+
         @pl.loop(0, chips)
         def _(k):
             fwd_arrival(it, k).wait_recv()
 
+        moved = arr[it] if it == 0 else arr[it] * power
         energy = jnp.zeros((8, LANES), F32)
         cross, square = energy, energy
         for g in range(groups):
             x = hid[2 * g : 2 * g + 2].reshape(256, slots)
-            p = dot(x, arr[it]) / n_rep
+            p = dot(x, moved) * rest
             energy = energy + fold(p * p)
             if it == 0:
                 cur1[2 * g : 2 * g + 2] = p.astype(BF16).reshape(2, LANES, columns)
             else:
-                prod[2 * g : 2 * g + 2] = p.reshape(2, LANES, columns)
+                out_ref[2 * g : 2 * g + 2] = p.reshape(2, LANES, columns)[:, :units]
                 c = cur1[2 * g : 2 * g + 2].reshape(256, columns).astype(F32) * scale
                 cross = cross + fold(c * p)
                 square = square + fold(c * c)
@@ -430,21 +450,16 @@
             + [jnp.zeros((5, LANES), F32)],
             axis=0,
         )
-        red_sib_copy(it).start()
-
-    reduce_z(1)
+        reduce_z(it)
+
     reduce_plane(1)
     total = reduce_end(1)
-    ray_ref[...] = jnp.broadcast_to(
-        total[1:2] / count / (total[2:3] / count + 1e-06), (8, LANES)
-    )
-    last = lax.rsqrt(total[0:1] / count + 1e-06)
-    for g in range(n_rep):
-        out_ref[g] = (prod[g, :units, :] * last).astype(BF16)
+    ray = total[1:2] / count / (total[2:3] / count + 1e-06)
+    ray_ref[0] = jnp.sum(ray)
+    scale_ref[0] = jnp.sum(lax.rsqrt(total[0:1] / count + 1e-06))
 
     @pl.loop(1, n_rep)
     def _(k):
-        rg_copy(k).wait_send()
         for it in range(ITERS):
             red_z_copy(it, k).wait_send()
 
@@ -452,8 +467,12 @@
         row_copy(way, step, q).wait_send()
         sib_copy(way, step, q).wait_send()
         hid_copy(way, step, q).wait_send()
+    for step, way in whole:
+        rg_copy(way, step).wait_send()
+    for step, q, way in passed:
+        pair_copy(way, step, q).wait_send()
+        sib_copy(way, step, q + 4).wait_send()
     for it in range(ITERS):
-        red_sib_copy(it).wait_send()
         for i in range(tiles):
             swap_copy(it, i).wait_send()
 
@@ -461,6 +480,9 @@
         def _(k):
             a2a_copy(it, lax.rem(chip + k, chips)).wait_send()
             back_copy(it, k).wait_send()
+
+        @pl.loop(1, n_ep)
+        def _(k):
             red_p_copy(it, k).wait_send()
 
         @pl.loop(0, chips)
@@ -479,18 +501,17 @@
     half = n_rep // 2
     width = depth // 2
     count = float(n_rep * n_ep * inner * columns)
-    rg = jnp.concatenate(
-        [routes.T.astype(F32), gates.T.astype(F32), jnp.zeros((4, tok), F32)], axis=0
-    )
     dma = pltpu.SemaphoreType.DMA
     per_expert = chips // EXPERTS
-    out, ray = pl.pallas_call(
+    out, scale, ray = pl.pallas_call(
         functools.partial(kernel, n_rep, n_ep, units, count),
         out_shape=(
-            jax.ShapeDtypeStruct((n_rep, units, columns), BF16),
-            jax.ShapeDtypeStruct((8, LANES), F32),
+            jax.ShapeDtypeStruct((n_rep, units, columns), F32),
+            jax.ShapeDtypeStruct((1,), F32),
+            jax.ShapeDtypeStruct((1,), F32),
         ),
         in_specs=[
+            pl.BlockSpec(memory_space=pltpu.VMEM),
             pl.BlockSpec(memory_space=pltpu.VMEM),
             pl.BlockSpec(memory_space=pltpu.VMEM),
             pl.BlockSpec(memory_space=pl.ANY),
@@ -499,7 +520,8 @@
         ],
         out_specs=(
             pl.BlockSpec(memory_space=pltpu.VMEM),
-            pl.BlockSpec(memory_space=pltpu.VMEM),
+            pl.BlockSpec(memory_space=pltpu.SMEM),
+            pl.BlockSpec(memory_space=pltpu.SMEM),
         ),
         scratch_shapes=[
             pltpu.VMEM((2 * LANES, depth), BF16),
@@ -511,37 +533,35 @@
             pltpu.VMEM((slots, n_rep * LANES), BF16),
             pltpu.VMEM((EXPERTS, tok, per_expert * CAP), BF16),
             pltpu.VMEM((EXPERTS * CAP, tok), BF16),
+            pltpu.VMEM((slots, LANES), F32),
             pltpu.VMEM((ITERS, slots, columns), F32),
             pltpu.VMEM((ITERS, slots, LANES), F32),
             pltpu.VMEM((ITERS, chips, CAP, LANES), BF16),
             pltpu.VMEM((ITERS, chips, CAP, LANES), BF16),
             pltpu.VMEM((ITERS, EXPERTS, CAP, LANES), BF16),
             pltpu.VMEM((ITERS, slots, columns), BF16),
-            pltpu.VMEM((n_rep, LANES, columns), F32),
-            pltpu.VMEM((ITERS, 8, LANES), F32),
-            pltpu.VMEM((ITERS, 8, LANES), F32),
             pltpu.VMEM((ITERS, 8, LANES), F32),
             pltpu.VMEM((ITERS, n_rep, 8, LANES), F32),
             pltpu.VMEM((ITERS, 8, LANES), F32),
-            pltpu.VMEM((ITERS, chips, 8, LANES), F32),
+            pltpu.VMEM((ITERS, n_ep, 8, LANES), F32),
             dma((3,)),
-            dma((2, n_rep)),
+            dma((2, 2, half)),
             dma((2, 2, half, PARTS)),
-            dma((2, 2, half, PARTS)),
+            dma((2, 2, half, 2)),
+            dma((2, 2, half, PARTS + 2)),
             dma((2, 2, half, PARTS)),
             dma((2, ITERS, max(1, slots // 256))),
             dma((2, ITERS, chips)),
             dma((2, ITERS, chips)),
             dma((2, ITERS, chips)),
-            dma((2, ITERS)),
             dma((2, ITERS, n_rep)),
-            dma((2, ITERS, chips)),
+            dma((2, ITERS, n_ep)),
         ],
         compiler_params=pltpu.CompilerParams(
             collective_id=0, has_side_effects=True, vmem_limit_bytes=56 * 2**20
         ),
-    )(rg, tokens, w_gate[0], w_up[0], direction[0].reshape(n_rep, units, columns))
-    return out.reshape(1, inner, columns), ray[0, :1]
+    )(routes.T, gates.T, tokens, w_gate[0], w_up[0], direction[0].reshape(n_rep, units, columns))
+    return (out * scale[0]).astype(BF16).reshape(1, inner, columns), ray
 
 
 def solution(mesh):

time: 185 us -> 165 us (0.89)
  Pallas kernels: 178 us -> 159 us
  local copies, waits for them, and re-layouts: 4.67 us -> 0 us
  other arithmetic: 0.67 us -> 3.26 us
    pallas_call x1, Pallas kernels: 178 us -> 159 us  [on_device(): pl.pallas_call(functools.partial(kernel, n_rep, n_ep, units, count), out_...]
    unnamed x5 -> x0, local copies, waits for them, and re-layouts: 3.41 us -> none
    convert_element_type x2 -> x1, other arithmetic: 0.01 us -> 3.26 us  [on_device(): return ((out * scale[0]).astype(BF16).reshape(1, inner, columns), ray)]
where the time goes in v2:
time: 165 us; the launch traced here: 164 us
  Pallas kernels  159 us (96%)
  other arithmetic  3.26 us (2%)
  between operations  2.46 us (1%)
    pallas_call x1, Pallas kernels, on_device(): pl.pallas_call(functools.partial(kernel, n_rep, n_ep, units, count), out_...  159 us

profile of v2, /device:TPU:1, one launch (start us, length us, event | category | flops | bytes accessed | tf_op | source)
XLA Modules:
  0.0 164.3 jit_solution(13564758315771799262)
XLA Ops:
  0.6 158.6 %shard_map.77 = (f32[16,112,256]{2,1,0:T(8,128)}, f32[1]{0:T(128)}, f32[1]{0:T(128)}) custom-call(s32[2,128]{1,0:T(2,128)} %bitcast.11, bf16[2,128]{1,0:T(2,128)(2,1)} %bitcast.12, bf16[128,4096]{1,0:T(8,128)(2,1)} %tok_ref.1, bf16[112,4096]{1,0:T(8,128)(2,1)} %bitcast.7, bf16[112,4096]{1,0:T(8,128)(2,1)} %bitcast.8, bf16[16,112,256]{2,1,0:T(8,128)(2,1)} %bitcast.9), custom_call_target="tpu_custom_call" | custom-call | tf_op jit(solution)/shard_map/pallas_call | solution.py:506
  159.2 3.3 %multiply_convert_fusion = bf16[16,112,256]{2,1,0:T(8,128)(2,1)} fusion(f32[16,112,256]{2,1,0:T(8,128)} %get-tuple-element.5, f32[]{:T(128)} %bitcast.5), kind=kLoop, calls=%fused_computation | loop fusion | flops 917504 | bytes 2752516 | tf_op jit(solution)/shard_map/convert_element_type | solution.py:564

commit v3 on v2

--- a/solution.py
+++ b/solution.py
@@ -1,4 +1,5 @@
 import functools
+import math
 
 import jax
 import jax.numpy as jnp
@@ -37,7 +38,7 @@
     rates, part, swap, snd, rcv, picks, arr,
     red_own, red_z, red_psrc, red_p,
     load_sem, rg_sem, row_sem, pair_sem, sib_sem, hid_sem, swap_sem, a2a_sem, back_sem, fwd_sem,
-    rz_sem, rp_sem,
+    rz_sem, rp_sem, near_sem,
 ):
     z = lax.axis_index("rep")
     ep = lax.axis_index("ep")
@@ -66,21 +67,29 @@
             device_id=device, device_id_type=pl.DeviceIdType.MESH,
         )
 
+    side = math.isqrt(chips)
+    at_y, at_x = chip // side, lax.rem(chip, side)
+    nearby = [
+        {"ep": (at_y * side + lax.rem(at_x + d, side)) * 2 + core} for d in (1, side - 1)
+    ] + [
+        {"ep": (lax.rem(at_y + d, side) * side + at_x) * 2 + core} for d in (1, side - 1)
+    ]
     barrier = pltpu.get_barrier_semaphore()
 
-    @pl.loop(1, n_rep)
-    def _(k):
+    def signal(sem, device):
         pl.semaphore_signal(
-            barrier, inc=1, device_id={"rep": lax.rem(z + k, n_rep)},
-            device_id_type=pl.DeviceIdType.MESH,
-        )
-
-    @pl.loop(1, n_ep)
-    def _(k):
-        pl.semaphore_signal(
-            barrier, inc=1, device_id={"ep": lax.rem(ep + k, n_ep)},
-            device_id_type=pl.DeviceIdType.MESH,
-        )
+            sem, inc=1, device_id=device, device_id_type=pl.DeviceIdType.MESH
+        )
+
+    for device in nearby + [sib] + [{"rep": lax.rem(z + d, n_rep)} for d in (1, n_rep - 1)]:
+        signal(barrier, device)
+
+    def greet(r):
+        for device in nearby:
+            signal(near_sem.at[r], device)
+
+    def met(r):
+        pl.semaphore_wait(near_sem.at[r], len(nearby))
 
     loads = [
         pltpu.make_async_copy(wg_ref, wcat.at[pl.ds(0, units)], load_sem.at[0]),
@@ -120,7 +129,8 @@
                 own_table, tok_ref[:, at : at + step_w]
             ).astype(BF16)
 
-    pl.semaphore_wait(barrier, n_rep - 1 + n_ep - 1)
+    pl.semaphore_wait(barrier, len(nearby) + 3)
+    greet(0)
 
     def block_at(way, step):
         return lax.rem(z + (n_rep - step if way == 0 else step), n_rep)
@@ -199,6 +209,10 @@
 
     late = list(passed)
     for step, q, way in order:
+        if (q, way) == (0, 0) and 2 <= step <= 4:
+            met(step - 2)
+            if step < 4:
+                greet(step - 1)
         row_arrival(way, step, q).wait_recv()
         if step < half and active(way, step + 1, q, half):
             row_copy(way, step + 1, q).start()
@@ -256,6 +270,19 @@
                 if active(way, 1, q, half):
                     hid_copy(way, 1, q).start()
 
+    def own_table_of(e):
+        t = slot_table(rgbuf[chip], jnp.float32(e))
+        table_t[e * CAP : (e + 1) * CAP, :] = t.astype(BF16)
+        tt = jnp.transpose(t, (1, 0))
+        table[e] = jnp.concatenate([tt] * per_expert, axis=1).astype(BF16)
+
+    def block_tangent(b, rows_at):
+        lanes = pl.ds(pl.multiple_of(b * LANES, LANES), LANES)
+        return dot(hid_t[rows_at, lanes], cur0[b])
+
+    for m in range(tiles):
+        rows_at = pl.ds(m * tile, tile)
+        part[0, rows_at] = block_tangent(z, rows_at)
     for step, q, way in order:
         hid_arrival(way, step, q).wait_recv()
         if step < half and active(way, step + 1, q, half):
@@ -265,6 +292,12 @@
         hid_t[q * hpiece : (q + 1) * hpiece, lanes] = jnp.transpose(
             hid[b, :, q * hpiece : (q + 1) * hpiece], (1, 0)
         )
+        if step < half:
+            rows_at = pl.ds(q * hpiece, hpiece)
+            part[0, rows_at] += block_tangent(b, rows_at)
+        if q == PARTS - 1 and way == 1:
+            for e in range(step - 1, EXPERTS, half):
+                own_table_of(e)
 
     def red_z_copy(it, k):
         b = lax.rem(z + k, n_rep)
@@ -368,12 +401,14 @@
 
     scale = None
     for it in range(ITERS):
-        source = cur0 if it == 0 else cur1
         for i in range(tiles):
             at = pl.ds(pl.multiple_of(tile_at(i) * tile, tile), tile)
-            part[it, at, :] = dot(
-                hid_t[at, :], source[...].reshape(n_rep * LANES, columns)
-            )
+            if it == 0:
+                part[0, at] += block_tangent(block_at(0, half), at)
+            else:
+                part[it, at, :] = dot(
+                    hid_t[at, :], cur1[...].reshape(n_rep * LANES, columns)
+                )
             swap_copy(it, i).start()
         for i in range(tiles):
             swap_copy(it, i).wait_recv()
@@ -385,14 +420,6 @@
                 rcv[it, chip] = snd[it, chip]
             for k in range(1 if i == 0 else 0, per_tile):
                 a2a_copy(it, m * per_tile + lax.rem(row_x + k, per_tile)).start()
-
-        if it == 0:
-            owned = rgbuf[chip]
-            for e in range(EXPERTS):
-                t = slot_table(owned, jnp.float32(e))
-                table_t[e * CAP : (e + 1) * CAP, :] = t.astype(BF16)
-                tt = jnp.transpose(t, (1, 0))
-                table[e] = jnp.concatenate([tt] * per_expert, axis=1).astype(BF16)
 
         @pl.loop(1, chips)
         def _(k):
@@ -556,6 +583,7 @@
             dma((2, ITERS, chips)),
             dma((2, ITERS, n_rep)),
             dma((2, ITERS, n_ep)),
+            pltpu.SemaphoreType.REGULAR((3,)),
         ],
         compiler_params=pltpu.CompilerParams(
             collective_id=0, has_side_effects=True, vmem_limit_bytes=56 * 2**20

time: 165 us -> 160 us (0.970)
  Pallas kernels: 159 us -> 154 us
    pallas_call x1, Pallas kernels: 159 us -> 154 us  [on_device(): pl.pallas_call(functools.partial(kernel, n_rep, n_ep, units, count), out_...]
where the time goes in v3:
time: 160 us; the launch traced here: 159 us
  Pallas kernels  154 us (96%)
  other arithmetic  3.26 us (2%)
  between operations  2.46 us (2%)
    pallas_call x1, Pallas kernels, on_device(): pl.pallas_call(functools.partial(kernel, n_rep, n_ep, units, count), out_...  154 us
    convert_element_type x1, other arithmetic, on_device(): return ((out * scale[0]).astype(BF16).reshape(1, inner, columns), ray)  3.26 us

profile of v3, /device:TPU:1, one launch (start us, length us, event | category | flops | bytes accessed | tf_op | source)
XLA Modules:
  0.0 159.4 jit_solution(11889007253001574617)
XLA Ops:
  0.6 153.7 %shard_map.77 = (f32[16,112,256]{2,1,0:T(8,128)}, f32[1]{0:T(128)}, f32[1]{0:T(128)}) custom-call(s32[2,128]{1,0:T(2,128)} %bitcast.11, bf16[2,128]{1,0:T(2,128)(2,1)} %bitcast.12, bf16[128,4096]{1,0:T(8,128)(2,1)} %tok_ref.1, bf16[112,4096]{1,0:T(8,128)(2,1)} %bitcast.7, bf16[112,4096]{1,0:T(8,128)(2,1)} %bitcast.8, bf16[16,112,256]{2,1,0:T(8,128)(2,1)} %bitcast.9), custom_call_target="tpu_custom_call" | custom-call | tf_op jit(solution)/shard_map/pallas_call | solution.py:533
  154.3 3.3 %multiply_convert_fusion = bf16[16,112,256]{2,1,0:T(8,128)(2,1)} fusion(f32[16,112,256]{2,1,0:T(8,128)} %get-tuple-element.5, f32[]{:T(128)} %bitcast.5), kind=kLoop, calls=%fused_computation | loop fusion | flops 917504 | bytes 2752516 | tf_op jit(solution)/shard_map/convert_element_type | solution.py:592

commit v4 on v3

--- a/solution.py
+++ b/solution.py
@@ -32,10 +32,10 @@
 
 def kernel(
     n_rep, n_ep, units, count,
-    routes_ref, gates_ref, tok_ref, wg_ref, wu_ref, dir_ref,
-    out_ref, scale_ref, ray_ref,
-    wcat, cur0, cur1, rows, rgbuf, hid, hid_t, table, table_t,
-    rates, part, swap, snd, rcv, picks, arr,
+    routes_ref, gates_ref, tok_hbm, wg_ref, wu_ref, dir_ref,
+    out_hbm, scale_ref, ray_ref,
+    wcat, cur0, gram, tang, rows, rgbuf, hid, hid_t, table, table_t,
+    rates, part, swap, snd, rcv, picks, arr, tok_ref, out_ref,
     red_own, red_z, red_psrc, red_p,
     load_sem, rg_sem, row_sem, pair_sem, sib_sem, hid_sem, swap_sem, a2a_sem, back_sem, fwd_sem,
     rz_sem, rp_sem, near_sem,
@@ -96,6 +96,8 @@
         pltpu.make_async_copy(wu_ref, wcat.at[pl.ds(LANES, units)], load_sem.at[1]),
         pltpu.make_async_copy(dir_ref, cur0.at[:, pl.ds(0, units)], load_sem.at[2]),
     ]
+    load_tokens = pltpu.make_async_copy(tok_hbm, tok_ref, load_sem.at[3])
+    load_tokens.start()
     for load in loads:
         load.start()
     pad = LANES - units
@@ -121,6 +123,7 @@
     )
     own_table = slot_table(own_rg, expert_f).astype(BF16)
     rgbuf[z] = own_rg
+    load_tokens.wait()
     step_w = min(512, width)
     for h in range(2):
         for k in range(width // step_w):
@@ -399,17 +402,34 @@
         s = jnp.sum(v.reshape(v.shape[0] // 8, 8, columns), axis=0)
         return s[:, :LANES] + s[:, LANES:]
 
+    def gram_tile(r):
+        at = slice(r * tile, (r + 1) * tile)
+        g = dot(hid_t[at], hid[...].reshape(n_rep * LANES, slots))
+        high = g.astype(BF16)
+        gram[0, at] = high
+        gram[1, at] = (g - high.astype(F32)).astype(BF16)
+
+    def lane_sum(v):
+        return jnp.sum(v, axis=0, keepdims=True)
+
+    first = max(1, tiles // 2)
     scale = None
     for it in range(ITERS):
+        energy = jnp.zeros((8, LANES), F32)
         for i in range(tiles):
             at = pl.ds(pl.multiple_of(tile_at(i) * tile, tile), tile)
             if it == 0:
                 part[0, at] += block_tangent(block_at(0, half), at)
             else:
-                part[it, at, :] = dot(
-                    hid_t[at, :], cur1[...].reshape(n_rep * LANES, columns)
-                )
+                back = (dot(gram[0, at], arr[0]) + dot(gram[1, at], arr[0])) / n_rep
+                part[it, at, :] = back
+                energy = energy + fold(back * arr[0, at].astype(F32)) / n_rep
             swap_copy(it, i).start()
+        if it == 1:
+            red_own[0] = jnp.concatenate(
+                [lane_sum(energy), jnp.zeros((7, LANES), F32)], axis=0
+            )
+            reduce_z(0)
         for i in range(tiles):
             swap_copy(it, i).wait_recv()
             m = tile_at(i)
@@ -421,6 +441,10 @@
             for k in range(1 if i == 0 else 0, per_tile):
                 a2a_copy(it, m * per_tile + lax.rem(row_x + k, per_tile)).start()
 
+        if it == 0:
+            for r in range(first):
+                gram_tile(r)
+
         @pl.loop(1, chips)
         def _(k):
             a2a_arrival(it, k).wait_recv()
@@ -431,6 +455,8 @@
                 per_expert * CAP, LANES
             )
             tangent = tangent + dot(table[e], got)
+        if it == 1:
+            tang[...] = tangent
         sent = tangent.astype(BF16)
         picks[it] = dot(table_t[...], sent).astype(BF16).reshape(EXPERTS, CAP, LANES)
         arr[it, slot_rows(chip), own_lanes] = picks[it, expert]
@@ -440,7 +466,10 @@
         def _(k):
             back_copy(it, k).start()
 
-        if it == 1:
+        if it == 0:
+            for r in range(first, tiles):
+                gram_tile(r)
+        else:
             reduce_plane(0)
 
         @pl.loop(1, chips)
@@ -448,40 +477,35 @@
             back_arrival(it, k).wait_recv()
             fwd_copy(it, k).start()
 
-        rest = 1.0 / n_rep
         if it == 1:
-            scale = lax.rsqrt(reduce_end(0)[0:1] / count + 1e-06)
+            mean = jnp.maximum(reduce_end(0)[0:1], 0.0) / count
+            scale = lax.rsqrt(mean + 1e-06)
             power = jnp.exp2(jnp.floor(jnp.log2(scale))).astype(BF16)
-            rest = scale / power.astype(F32) * rest
+            rest = scale / power.astype(F32) / n_rep
+            t = tang[...] * scale
+            cross = lane_sum(t * (tang[...].astype(BF16).astype(F32) * scale)) / n_rep
 
         @pl.loop(0, chips)
         def _(k):
             fwd_arrival(it, k).wait_recv()
 
-        moved = arr[it] if it == 0 else arr[it] * power
-        energy = jnp.zeros((8, LANES), F32)
-        cross, square = energy, energy
-        for g in range(groups):
-            x = hid[2 * g : 2 * g + 2].reshape(256, slots)
-            p = dot(x, moved) * rest
-            energy = energy + fold(p * p)
-            if it == 0:
-                cur1[2 * g : 2 * g + 2] = p.astype(BF16).reshape(2, LANES, columns)
-            else:
-                out_ref[2 * g : 2 * g + 2] = p.reshape(2, LANES, columns)[:, :units]
-                c = cur1[2 * g : 2 * g + 2].reshape(256, columns).astype(F32) * scale
-                cross = cross + fold(c * p)
-                square = square + fold(c * c)
-        red_own[it] = jnp.concatenate(
-            [jnp.sum(v, axis=0, keepdims=True) for v in (energy, cross, square)]
-            + [jnp.zeros((5, LANES), F32)],
-            axis=0,
-        )
-        reduce_z(it)
-
+    moved = arr[1] * power
+    energy = jnp.zeros((8, LANES), F32)
+    for g in range(groups):
+        x = hid[2 * g : 2 * g + 2].reshape(256, slots)
+        p = dot(x, moved) * rest
+        energy = energy + fold(p * p)
+        out_ref[2 * g : 2 * g + 2] = p.reshape(2, LANES, columns)[:, :units]
+    red_own[1] = jnp.concatenate(
+        [lane_sum(energy), cross, jnp.zeros((6, LANES), F32)], axis=0
+    )
+    reduce_z(1)
+    store = pltpu.make_async_copy(out_ref, out_hbm, load_sem.at[4])
+    store.start()
     reduce_plane(1)
     total = reduce_end(1)
-    ray = total[1:2] / count / (total[2:3] / count + 1e-06)
+    store.wait()
+    ray = total[1:2] / count / (scale * scale * mean + 1e-06)
     ray_ref[0] = jnp.sum(ray)
     scale_ref[0] = jnp.sum(lax.rsqrt(total[0:1] / count + 1e-06))
 
@@ -540,20 +564,21 @@
         in_specs=[
             pl.BlockSpec(memory_space=pltpu.VMEM),
             pl.BlockSpec(memory_space=pltpu.VMEM),
-            pl.BlockSpec(memory_space=pltpu.VMEM),
+            pl.BlockSpec(memory_space=pl.ANY),
             pl.BlockSpec(memory_space=pl.ANY),
             pl.BlockSpec(memory_space=pl.ANY),
             pl.BlockSpec(memory_space=pl.ANY),
         ],
         out_specs=(
-            pl.BlockSpec(memory_space=pltpu.VMEM),
+            pl.BlockSpec(memory_space=pl.ANY),
             pl.BlockSpec(memory_space=pltpu.SMEM),
             pl.BlockSpec(memory_space=pltpu.SMEM),
         ),
         scratch_shapes=[
             pltpu.VMEM((2 * LANES, depth), BF16),
             pltpu.VMEM((n_rep, LANES, columns), BF16),
-            pltpu.VMEM((n_rep, LANES, columns), BF16),
+            pltpu.VMEM((2, slots, slots), BF16),
+            pltpu.VMEM((tok, LANES), F32),
             pltpu.VMEM((2, n_rep, CAP, width), BF16),
             pltpu.VMEM((n_rep, 8, tok), F32),
             pltpu.VMEM((n_rep, LANES, slots), BF16),
@@ -567,11 +592,13 @@
             pltpu.VMEM((ITERS, chips, CAP, LANES), BF16),
             pltpu.VMEM((ITERS, EXPERTS, CAP, LANES), BF16),
             pltpu.VMEM((ITERS, slots, columns), BF16),
+            pltpu.VMEM((tok, depth), BF16),
+            pltpu.VMEM((n_rep, units, columns), F32),
             pltpu.VMEM((ITERS, 8, LANES), F32),
             pltpu.VMEM((ITERS, n_rep, 8, LANES), F32),
             pltpu.VMEM((ITERS, 8, LANES), F32),
             pltpu.VMEM((ITERS, n_ep, 8, LANES), F32),
-            dma((3,)),
+            dma((5,)),
             dma((2, 2, half)),
             dma((2, 2, half, PARTS)),
             dma((2, 2, half, 2)),

time: 160 us -> 157 us (0.981)
  Pallas kernels: 154 us -> 151 us
    pallas_call x1, Pallas kernels: 154 us -> 151 us  [on_device(): pl.pallas_call(functools.partial(kernel, n_rep, n_ep, units, count), out_...]
where the time goes in v4:
time: 157 us
  Pallas kernels  151 us (96%)
  other arithmetic  3.26 us (2%)
  between operations  2.46 us (2%)
    pallas_call x1, Pallas kernels, on_device(): pl.pallas_call(functools.partial(kernel, n_rep, n_ep, units, count), out_...  151 us
    convert_element_type x1, other arithmetic, on_device(): return ((out * scale[0]).astype(BF16).reshape(1, inner, columns), ray)  3.26 us

profile of v4, /device:TPU:1, one launch (start us, length us, event | category | flops | bytes accessed | tf_op | source)
XLA Modules:
  0.0 156.7 jit_solution(1698288201629611419)
XLA Ops:
  0.6 151.0 %shard_map.77 = (f32[16,112,256]{2,1,0:T(8,128)}, f32[1]{0:T(128)}, f32[1]{0:T(128)}) custom-call(s32[2,128]{1,0:T(2,128)} %bitcast.11, bf16[2,128]{1,0:T(2,128)(2,1)} %bitcast.12, bf16[128,4096]{1,0:T(8,128)(2,1)} %tok_hbm.1, bf16[112,4096]{1,0:T(8,128)(2,1)} %bitcast.7, bf16[112,4096]{1,0:T(8,128)(2,1)} %bitcast.8, bf16[16,112,256]{2,1,0:T(8,128)(2,1)} %bitcast.9), custom_call_target="tpu_custom_call" | custom-call | tf_op jit(solution)/shard_map/pallas_call | solution.py:557
  151.6 3.3 %multiply_convert_fusion = bf16[16,112,256]{2,1,0:T(8,128)(2,1)} fusion(f32[16,112,256]{2,1,0:T(8,128)} %get-tuple-element.5, f32[]{:T(128)} %bitcast.5), kind=kLoop, calls=%fused_computation | loop fusion | flops 917504 | bytes 2752516 | tf_op jit(solution)/shard_map/convert_element_type | solution.py:619
